TPU v7x, 512 devices: a whole 4x8x8 slice. The times are simulated.
512 devices in a mesh: row: 16 (over z_lo, x), col: 32 (over z_hi, y, core).
Axes of the slice: x: 4, y: 8, z: 8 (z_hi: 2, z_lo: 4; z = z_hi * 4 + z_lo), core: 2. Of those that a mesh axis runs over, the one named last changes fastest.
Arguments:
- values: float32 [8192, 8192], P('col', 'row'), may hold values from 0.01 to 100, as said below
- pattern: int32 [64, 64], replicated, may hold values from 0 to 1, as said below
- prune: int32 [64, 64], P('col', 'row'), may hold values from 0 to 1, as said below
Outputs:
- clustered: float32 [8192, 8192], P('col', 'row')
Inputs may be any that keep to these rules, and one draw needn't show every extreme that they name: `values`: all positive. `pattern`: every diagonal tile is 1. A block is the tiles of rows a * 2 to a * 2 + 1 and columns b * 4 to b * 4 + 3; every block holds at most 2 ones, and for some a every block of block row a, and for some b every block of block column b, holds exactly 2. `prune`: every diagonal tile is 1.
All inputs are finite; a program needn't handle non-finite values.
Results may differ from a plain program's by a relative error of at most 0.0015.
Values may be sent and summed in bfloat16 or wider, within the bound.
A program may use at most 64 MiB of HBM per device.

v0:
```python
import jax
import jax.numpy as jnp
from jax import lax
from jax.sharding import PartitionSpec as P

TILE = 128


def expand(mask):
    wide = jnp.repeat(mask.astype(jnp.float32), TILE, axis=0)
    return jnp.repeat(wide, TILE, axis=1)


def on_device(values, pattern, prune):
    tile_rows = prune.shape[0]
    tile_cols = prune.shape[1]
    own_row = lax.axis_index("col")
    own_col = lax.axis_index("row")
    own_pattern = lax.dynamic_slice(
        pattern, (own_row * tile_rows, own_col * tile_cols), (tile_rows, tile_cols)
    )
    masked = values * expand(own_pattern)
    in_total = lax.psum(jnp.sum(masked, axis=0), "col")
    stoch = (masked / in_total[None, :]).astype(jnp.bfloat16)
    height, breadth = stoch.shape
    column_panel = lax.all_gather(stoch, "col", axis=0, tiled=True)
    square = jnp.dot(
        lax.all_gather(stoch, "row", axis=1, tiled=True),
        column_panel,
        preferred_element_type=jnp.float32,
    )
    inflated = square * square * expand(prune)
    out_total = lax.psum(jnp.sum(inflated, axis=0), "col")
    matrix_order = height * lax.axis_size("col")
    return matrix_order * inflated / out_total[None, :]


def solution(mesh):
    in_specs = (P("col", "row"), P(), P("col", "row"))
    out_specs = P("col", "row")
    return jax.shard_map(
        on_device, mesh=mesh, in_specs=in_specs, out_specs=out_specs, check_vma=False
    )
```

profile of v0, /device:TPU:1, one launch (start us, length us, event | category | flops | bytes accessed | tf_op | source)
XLA Modules:
  0.0 427.4 jit_solution(13993588111448434464)
XLA Ops:
  6.5 0.0 all-gather.3.cloned.1.call-start
  6.5 0.8 dynamic-slice_convert_fusion
  7.3 0.3 broadcast_in_dim.15
  7.6 1.1 fusion.1
  8.8 90.5 %psum.14 = f32[512]{0:T(512)S(1)} all-reduce(f32[512]{0:T(512)S(1)} %fusion.1), channel_id=1, replica_groups=mesh['row'=16,'col'=32] {'col'}, use_global_device_ids=true, to_apply=%region_1.0 | all-reduce | flops 512 | bytes 4096 | tf_op jit(solution)/shard_map/psum | solution.py:23
  99.2 1.8 divide_convert_fusion
  101.1 0.0 all-gather.3.cloned.1.call-update
  101.1 0.0 all-gather.5.cloned.1.call-start
  101.2 0.7 all-gather.5.cloned.1.call-update
  101.9 0.7 convert_element_type.11
  102.6 80.5 %all-gather.3.cloned.1.call-done = bf16[256,8192]{1,0:T(8,128)(2,1)} async-done(((bf16[256,512]{1,0:T(8,128)(2,1)}), bf16[256,8192]{1,0:T(8,128)(2,1)}) %all-gather.3.cloned.1.call-update) | async-done | bytes 4194320 | tf_op jit(solution)/shard_map/all_gather | solution.py:28
  183.0 145.4 %all-gather.5.cloned.1.call-done = bf16[8192,512]{1,0:T(8,128)(2,1)} async-done(((bf16[256,512]{1,0:T(8,128)(2,1)}), bf16[8192,512]{1,0:T(8,128)(2,1)}) %all-gather.5.cloned.1.call-update) | async-done | bytes 8388624 | tf_op jit(solution)/shard_map/all_gather | solution.py:26
  328.4 0.3 broadcast_in_dim.17
  328.8 7.0 %fusion.2 = (f32[512]{0:T(512)S(1)}, f32[256,512]{1,0:T(8,128)S(1)}) fusion(f32[32,8,4,128]{3,2,1,0:T(4,128)S(1)} %bitcast.16, bf16[256,8192]{1,0:T(8,128)(2,1)} %all-gather.3.cloned.1.call-done, bf16[8192,512]{1,0:T(8,128)(2,1)} %all-gather.5.cloned.1.call-done), kind=kOutput, calls=%fused_computation.7 | convolution fusion | flops 2147876352 | bytes 13633536 | tf_op jit(solution)/shard_map/dot_general | solution.py:27
  335.8 83.9 %psum.15 = f32[512]{0:T(512)S(1)} all-reduce(f32[512]{0:T(512)S(1)} %get-tuple-element.5), channel_id=1, replica_groups=mesh['row'=16,'col'=32] {'col'}, use_global_device_ids=true, to_apply=%region_3.0 | all-reduce | flops 512 | bytes 4096 | tf_op jit(solution)/shard_map/psum | solution.py:33
  419.7 0.9 multiply_divide_fusion
  (2 shorter events, 0.0 us)
Async XLA Ops:
  6.5 176.5 %all-gather.3.cloned.1.call-start = ((), (), s32[]{:S(2)}) async-start(), calls=%async_computation | async-start | bytes 4456448 | tf_op jit(solution)/shard_map/all_gather | solution.py:28
  101.1 227.3 %all-gather.5.cloned.1.call-start = ((), (), s32[]{:S(2)}) async-start(), calls=%async_computation.1 | async-start | bytes 8650752 | tf_op jit(solution)/shard_map/all_gather | solution.py:26
Sparse Core Ops, SparseCore 0:
  101.2 81.7 all-gather.2
  186.4 142.0 all-gather.4
where the time goes:
time: 428 us; the launch traced here: 427 us
  waiting for transfers between devices  227 us (53%)
  blocking collectives  174 us (41%)
  between operations  13.4 us (3%)
  matrix products  7 us (2%)
  other arithmetic  5.29 us (1%)
    all_gather x1, waiting for transfers between devices, on_device(): column_panel = lax.all_gather(stoch, 'col', axis=0, tiled=True)  145 us
    psum x1, blocking collectives, on_device(): in_total = lax.psum(jnp.sum(masked, axis=0), 'col')  90.5 us
    psum x1, blocking collectives, on_device(): out_total = lax.psum(jnp.sum(inflated, axis=0), 'col')  83.9 us
    all_gather x1, waiting for transfers between devices, on_device(): lax.all_gather(stoch, 'row', axis=1, tiled=True)  80.5 us
  transfers between devices with their start and end apart: 2, of which 2 were waited for; matrix products, arithmetic and copies ran while one was open for 0% of the time, Pallas kernels for 0%

commit v1 on v0

v1 whole, which is shorter than its diff:
```python
import functools

import jax
import jax.numpy as jnp
from jax import lax
from jax.experimental import pallas as pl
from jax.experimental.pallas import tpu as pltpu
from jax.sharding import PartitionSpec as P

TILE = 128
SLOTS = 2
CORES = 2
Z_HI = 2
Z_LO = 4


def kernel(
    rows,
    cols,
    values_hbm,
    pattern,
    prune,
    out_hbm,
    values,
    a_pack,
    b_pack,
    in_own,
    in_parts,
    in_total,
    out_own,
    out_parts,
    result,
    b_slot,
    a_row,
    a_col,
    load_sem,
    store_sem,
    in_send,
    in_recv,
    out_send,
    out_recv,
    a_send,
    a_recv,
    b_send,
    b_recv,
):
    tr, tc = prune.shape
    x_size = rows // Z_LO
    y_size = cols // (CORES * Z_HI)
    r, c = lax.axis_index("row"), lax.axis_index("col")
    zl, x = r // x_size, r % x_size
    core = c % CORES
    y = (c // CORES) % y_size
    zh = c // (CORES * y_size)

    def row_of(zl_, x_):
        return zl_ * x_size + x_

    def col_of(zh_, y_, core_):
        return (zh_ * y_size + y_) * CORES + core_

    loads = [
        pltpu.make_async_copy(
            values_hbm.at[pl.ds(t // tc * TILE, TILE), pl.ds(t % tc * TILE, TILE)],
            values.at[t],
            load_sem.at[t],
        )
        for t in range(tr * tc)
    ]
    for load in loads:
        load.start()

    barrier = pltpu.get_barrier_semaphore()

    def greet_col(d, carry):
        pl.semaphore_signal(barrier, inc=1, device_id={"col": (c + d) % cols})
        return carry

    lax.fori_loop(1, cols, greet_col, 0)
    row_peers = [row_of((zl + d) % Z_LO, x) for d in range(1, Z_LO)]
    row_peers += [row_of(zl, (x + d) % x_size) for d in range(1, x_size)]
    for peer in row_peers:
        pl.semaphore_signal(barrier, inc=1, device_id={"row": peer})

    seen = jnp.int32(0)
    place = [jnp.int32(0)] * SLOTS
    place_col = [jnp.int32(0)] * SLOTS
    for t in range(tr * tc):
        here = pattern[tr * c + t // tc, tc * r + t % tc]
        for s in range(SLOTS):
            hit = (here > 0) & (seen == s)
            place[s] = jnp.where(hit, t, place[s])
            place_col[s] = jnp.where(hit, t % tc, place_col[s])
        seen = seen + here

    for load in loads:
        load.wait()
    tiles = []
    partial = [jnp.zeros((1, TILE), jnp.float32) for _ in range(tc)]
    for s in range(SLOTS):
        tile = jnp.where(seen > s, values[place[s]], 0.0)
        tiles.append(tile)
        total = jnp.sum(tile, axis=0, keepdims=True)
        for j in range(tc):
            partial[j] = partial[j] + jnp.where(place_col[s] == j, total, 0.0)
    in_own[...] = jnp.concatenate(partial, axis=1)

    pl.semaphore_wait(barrier, cols - 1 + len(row_peers))

    def exchange(own_ref, parts_ref, send_sem, recv_sem):
        def send(d, carry):
            pltpu.make_async_remote_copy(
                src_ref=own_ref,
                dst_ref=parts_ref.at[cols - 1 - d],
                send_sem=send_sem,
                recv_sem=recv_sem,
                device_id={"col": (c + d) % cols},
            ).start()
            return carry

        lax.fori_loop(1, cols, send, 0)

    def collect(own_ref, parts_ref, recv_sem):
        pltpu.make_async_copy(parts_ref, parts_ref, recv_sem).wait()
        return own_ref[...] + jnp.sum(parts_ref[...], axis=0)

    def drain(parts_ref, send_sem):
        pltpu.make_async_copy(parts_ref, parts_ref, send_sem).wait()

    exchange(in_own, in_parts, in_send, in_recv)
    in_sum = collect(in_own, in_parts, in_recv)
    for j in range(tc):
        in_total[j] = in_sum[:, j * TILE : (j + 1) * TILE]
    for s in range(SLOTS):
        stoch = (tiles[s] / in_total[place_col[s]]).astype(jnp.bfloat16)
        a_pack[SLOTS * r + s] = stoch
        b_pack[SLOTS * c + s] = stoch
    b_pack[SLOTS * cols] = jnp.zeros((TILE, TILE), jnp.bfloat16)

    a_count, b_count = 0, 0

    def packed(ref, origin):
        return ref.at[pl.ds(SLOTS * origin, SLOTS)]

    def arrived(ref, origin, sem):
        pltpu.make_async_copy(packed(ref, origin), packed(ref, origin), sem).wait()

    def send_a(origin, peer):
        nonlocal a_count
        pltpu.make_async_remote_copy(
            src_ref=packed(a_pack, origin),
            dst_ref=packed(a_pack, origin),
            send_sem=a_send.at[a_count],
            recv_sem=a_recv.at[origin],
            device_id={"row": peer},
        ).start()
        a_count += 1

    def send_b(origin, peer):
        nonlocal b_count
        pltpu.make_async_remote_copy(
            src_ref=packed(b_pack, origin),
            dst_ref=packed(b_pack, origin),
            send_sem=b_send.at[b_count],
            recv_sem=b_recv.at[origin],
            device_id={"col": peer},
        ).start()
        b_count += 1

    def wait_a(origin):
        arrived(a_pack, origin, a_recv.at[origin])

    def wait_b(origin):
        arrived(b_pack, origin, b_recv.at[origin])

    sibling = col_of(zh, y, 1 - core)
    up = col_of(zh, (y + 1) % y_size, core)
    down = col_of(zh, (y + y_size - 1) % y_size, core)
    other = 1 - zh
    half = y_size // 2

    def around_x(origin):
        for d in (1, x_size - 1, *range(2, x_size - 1)):
            send_a(origin, row_of(zl, (x + d) % x_size))

    send_b(c, up)
    send_b(c, down)
    around_x(r)
    send_b(c, col_of(other, y, core))
    for d in range(1, Z_LO):
        send_a(r, row_of((zl + d) % Z_LO, x))
    send_b(c, sibling)

    def locate_b(block, carry):
        count = jnp.int32(0)
        for t in range(tr * tc):
            here = pattern[tr * block + t // tc, tc * r + t % tc]
            b_slot[block * tr * tc + t] = jnp.where(here > 0, SLOTS * block + count, SLOTS * cols)
            count = count + here
        return carry

    lax.fori_loop(0, cols, locate_b, 0)

    def locate_a(block, carry):
        count = jnp.int32(0)
        row_ = [jnp.int32(tr)] * SLOTS
        col_ = [jnp.int32(0)] * SLOTS
        for t in range(tr * tc):
            here = pattern[tr * c + t // tc, tc * block + t % tc]
            for s in range(SLOTS):
                hit = (here > 0) & (count == s)
                row_[s] = jnp.where(hit, t // tc, row_[s])
                col_[s] = jnp.where(hit, t % tc, col_[s])
            count = count + here
        for s in range(SLOTS):
            a_row[block * SLOTS + s] = row_[s]
            a_col[block * SLOTS + s] = tc * (tc * block + col_[s])
        return carry

    lax.fori_loop(0, rows, locate_a, 0)

    def pass_on(origin, peer, last):
        wait_b(origin)
        if not last:
            send_b(origin, peer)
        send_b(origin, sibling)

    for step in range(1, half + 1):
        pass_on(col_of(zh, (y + y_size - step) % y_size, core), up, step == half)
        if step < half:
            pass_on(col_of(zh, (y + step) % y_size, core), down, step == half - 1)
        if step < Z_LO:
            origin = row_of((zl + step) % Z_LO, x)
            wait_a(origin)
            around_x(origin)
        if step == 1:
            origin = col_of(other, y, core)
            wait_b(origin)
            send_b(origin, up)
            send_b(origin, down)
            send_b(origin, sibling)
        else:
            pass_on(col_of(other, (y + y_size - step + 1) % y_size, core), up, step == half)
            pass_on(col_of(other, (y + step - 1) % y_size, core), down, False)
    pass_on(col_of(other, (y + half) % y_size, core), down, True)

    for zl_ in range(Z_LO):
        for d in range(1, x_size):
            wait_a(row_of((zl + zl_) % Z_LO, (x + d) % x_size))

    def wait_sibling(block, carry):
        wait_b(block * CORES + 1 - core)
        return carry

    lax.fori_loop(0, cols // CORES, wait_sibling, 0)

    result[...] = jnp.zeros_like(result)

    def multiply(block, carry):
        left, right = [], []
        for s in range(SLOTS):
            row_ = a_row[block * SLOTS + s]
            k = a_col[block * SLOTS + s]
            tile = a_pack[block * SLOTS + s]
            left.append(
                jnp.concatenate(
                    [jnp.where(row_ == i, tile, jnp.zeros_like(tile)) for i in range(tr)], axis=0
                )
            )
            right.append(jnp.concatenate([b_pack[b_slot[k + j]] for j in range(tc)], axis=1))
        result[...] += jnp.dot(
            jnp.concatenate(left, axis=1),
            jnp.concatenate(right, axis=0),
            preferred_element_type=jnp.float32,
        )
        return carry

    lax.fori_loop(0, rows, multiply, 0)

    sums = []
    for j in range(tc):
        col_sum = jnp.zeros((1, TILE), jnp.float32)
        for i in range(tr):
            at = (slice(i * TILE, (i + 1) * TILE), slice(j * TILE, (j + 1) * TILE))
            square = result[at]
            inflated = jnp.where(prune[i, j] > 0, square * square, 0.0)
            result[at] = inflated
            col_sum = col_sum + jnp.sum(inflated, axis=0, keepdims=True)
        sums.append(col_sum)
    out_own[...] = jnp.concatenate(sums, axis=1)

    exchange(out_own, out_parts, out_send, out_recv)
    drain(in_parts, in_send)
    for n in range(a_count):
        arrived(a_pack, 0, a_send.at[n])
    for n in range(b_count):
        arrived(b_pack, 0, b_send.at[n])
    out_sum = collect(out_own, out_parts, out_recv)
    order = tr * TILE * cols
    result[...] = result[...] * (order / out_sum)
    store = pltpu.make_async_copy(result, out_hbm, store_sem)
    store.start()
    drain(out_parts, out_send)
    store.wait()


def on_device(rows, cols, values, pattern, prune):
    tr, tc = prune.shape
    height, width = values.shape
    f32, bf16 = jnp.float32, jnp.bfloat16
    dma = pltpu.SemaphoreType.DMA
    return pl.pallas_call(
        functools.partial(kernel, rows, cols),
        out_shape=jax.ShapeDtypeStruct((height, width), f32),
        in_specs=[
            pl.BlockSpec(memory_space=pl.ANY),
            pl.BlockSpec(memory_space=pltpu.SMEM),
            pl.BlockSpec(memory_space=pltpu.SMEM),
        ],
        out_specs=pl.BlockSpec(memory_space=pl.ANY),
        scratch_shapes=[
            pltpu.VMEM((tr * tc, TILE, TILE), f32),
            pltpu.VMEM((rows * SLOTS, TILE, TILE), bf16),
            pltpu.VMEM((cols * SLOTS + 1, TILE, TILE), bf16),
            pltpu.VMEM((1, width), f32),
            pltpu.VMEM((cols - 1, 1, width), f32),
            pltpu.VMEM((tc, 1, TILE), f32),
            pltpu.VMEM((1, width), f32),
            pltpu.VMEM((cols - 1, 1, width), f32),
            pltpu.VMEM((height, width), f32),
            pltpu.SMEM((cols * tr * tc,), jnp.int32),
            pltpu.SMEM((rows * SLOTS,), jnp.int32),
            pltpu.SMEM((rows * SLOTS,), jnp.int32),
            dma((tr * tc,)),
            dma,
            dma,
            dma,
            dma,
            dma,
            dma((rows,)),
            dma((rows,)),
            dma((cols,)),
            dma((cols,)),
        ],
        compiler_params=pltpu.CompilerParams(
            collective_id=0,
            has_side_effects=True,
            vmem_limit_bytes=32 * 1024 * 1024,
        ),
        cost_estimate=pl.CostEstimate(
            flops=2 * height * width * TILE * SLOTS * rows,
            bytes_accessed=2 * 4 * height * width,
            transcendentals=0,
        ),
    )(values, pattern, prune)


def solution(mesh):
    in_specs = (P("col", "row"), P(), P("col", "row"))
    out_specs = P("col", "row")
    return jax.shard_map(
        functools.partial(on_device, mesh.shape["row"], mesh.shape["col"]),
        mesh=mesh,
        in_specs=in_specs,
        out_specs=out_specs,
        check_vma=False,
    )
```

time: 428 us -> 64.2 us (0.15)
  waiting for transfers between devices: 227 us -> 0 us
  blocking collectives: 174 us -> 0 us
  Pallas kernels: 0 us -> 60.4 us
  between operations: 13.4 us -> 0.01 us
  matrix products: 7 us -> 0 us
  other arithmetic: 5.29 us -> 0 us
    all_gather x2 -> x0, waiting for transfers between devices: 226 us -> none  [the longest x1 145 us: on_device(): column_panel = lax.all_gather(stoch, 'col', axis=0, tiled=True)]
    psum x2 -> x0, blocking collectives: 174 us -> none  [the longest x1 90.5 us: on_device(): in_total = lax.psum(jnp.sum(masked, axis=0), 'col')]
    pallas_call x0 -> x1, Pallas kernels: none -> 60.4 us  [on_device(): pl.pallas_call(functools.partial(kernel, rows, cols), out_shape=jax.Shape...]
    dot_general x1 -> x0, matrix products: 7 us -> none  [on_device(): jnp.dot(lax.all_gather(stoch, 'row', axis=1, tiled=True), column_panel, p...]
  transfers between devices with their start and end apart: 2 -> 0, of which waited for: 2 -> 0; matrix products, arithmetic and copies ran while one was open for 0% -> 0% of each run, Pallas kernels for 0% -> 0%
where the time goes in v1:
time: 64.2 us; the launch traced here: 63.7 us
  Pallas kernels  60.4 us (94%)
  local copies, waits for them, and re-layouts  3.27 us (5%)
    pallas_call x1, Pallas kernels, on_device(): pl.pallas_call(functools.partial(kernel, rows, cols), out_shape=jax.Shape...  60.4 us
    unnamed x7, local copies, waits for them, and re-layouts  3.27 us

profile of v1, /device:TPU:1, one launch (start us, length us, event | category | flops | bytes accessed | tf_op | source)
XLA Modules:
  0.0 63.7 jit_solution(5942876698026456442)
XLA Ops:
  0.0 0.0 copy-start
  0.0 1.0 %copy-done = f32[256,512]{1,0:T(8,128)S(1)} copy-done((f32[256,512]{1,0:T(8,128)S(1)}, f32[256,512]{1,0:T(8,128)}, u32[]{:S(2)}) %copy-start) | copy-done | bytes 524312
  1.0 0.0 copy-start.1
  1.0 0.8 %copy-done.1 = s32[64,64]{1,0:T(8,128)S(1)} copy-done((s32[64,64]{1,0:T(8,128)S(1)}, s32[64,64]{1,0:T(8,128)}, u32[]{:S(2)}) %copy-start.1) | copy-done | bytes 16408
  1.8 0.0 copy-start.2
  1.8 0.7 %copy-done.2 = s32[2,4]{1,0:T(2,128)S(1)} copy-done((s32[2,4]{1,0:T(2,128)S(1)}, s32[2,4]{1,0:T(2,128)}, u32[]{:S(2)}) %copy-start.2) | copy-done | bytes 56
  2.5 60.4 %shard_map.37 = f32[256,512]{1,0:T(8,128)S(1)} custom-call(f32[256,512]{1,0:T(8,128)S(1)} %copy-done, s32[64,64]{1,0:T(8,128)S(1)} %copy-done.1, s32[2,4]{1,0:T(2,128)S(1)} %copy-done.2), custom_call_target="tpu_custom_call" | custom-call | flops 1073741824 | bytes 1048576 | tf_op jit(solution)/shard_map/pallas_call | solution.py:312
  62.9 0.8 %copy.5 = f32[256,512]{1,0:T(8,128)} copy(f32[256,512]{1,0:T(8,128)S(1)} %shard_map.37) | data formatting | bytes 1048576
Async XLA Ops:
  0.0 1.0 %copy-start = (f32[256,512]{1,0:T(8,128)S(1)}, f32[256,512]{1,0:T(8,128)}, u32[]{:S(2)}) copy-start(f32[256,512]{1,0:T(8,128)} %values_hbm.1) | copy-start | bytes 1572868
  1.0 0.8 %copy-start.1 = (s32[64,64]{1,0:T(8,128)S(1)}, s32[64,64]{1,0:T(8,128)}, u32[]{:S(2)}) copy-start(s32[64,64]{1,0:T(8,128)} %pattern.1) | copy-start | bytes 49156
  1.8 0.7 %copy-start.2 = (s32[2,4]{1,0:T(2,128)S(1)}, s32[2,4]{1,0:T(2,128)}, u32[]{:S(2)}) copy-start(s32[2,4]{1,0:T(2,128)} %prune.1) | copy-start | bytes 100

commit v2 on v1

--- a/solution.py
+++ b/solution.py
@@ -18,10 +18,16 @@
     rows,
     cols,
     values_hbm,
+    pattern_hbm,
+    prune_hbm,
+    result_hbm,
+    scale_hbm,
+    values,
     pattern,
     prune,
-    out_hbm,
-    values,
+    raw_own,
+    raw_other,
+    scale,
     a_pack,
     b_pack,
     in_own,
@@ -35,6 +41,10 @@
     a_col,
     load_sem,
     store_sem,
+    fetch_sem,
+    raw_sem,
+    far_send,
+    far_recv,
     in_send,
     in_recv,
     out_send,
@@ -67,8 +77,12 @@
         )
         for t in range(tr * tc)
     ]
-    for load in loads:
-        load.start()
+    fetches = [
+        pltpu.make_async_copy(pattern_hbm, pattern, fetch_sem.at[0]),
+        pltpu.make_async_copy(prune_hbm, prune, fetch_sem.at[1]),
+    ]
+    for copy in fetches + loads:
+        copy.start()
 
     barrier = pltpu.get_barrier_semaphore()
 
@@ -82,24 +96,31 @@
     for peer in row_peers:
         pl.semaphore_signal(barrier, inc=1, device_id={"row": peer})
 
-    seen = jnp.int32(0)
-    place = [jnp.int32(0)] * SLOTS
-    place_col = [jnp.int32(0)] * SLOTS
-    for t in range(tr * tc):
-        here = pattern[tr * c + t // tc, tc * r + t % tc]
-        for s in range(SLOTS):
-            hit = (here > 0) & (seen == s)
-            place[s] = jnp.where(hit, t, place[s])
-            place_col[s] = jnp.where(hit, t % tc, place_col[s])
-        seen = seen + here
-
-    for load in loads:
-        load.wait()
+    for copy in fetches:
+        copy.wait()
+
+    def locate(block_row, block_col):
+        seen = jnp.int32(0)
+        place = [jnp.int32(0)] * SLOTS
+        place_col = [jnp.int32(0)] * SLOTS
+        for t in range(tr * tc):
+            here = pattern[tr * block_row + t // tc, tc * block_col + t % tc]
+            for s in range(SLOTS):
+                hit = (here > 0) & (seen == s)
+                place[s] = jnp.where(hit, t, place[s])
+                place_col[s] = jnp.where(hit, t % tc, place_col[s])
+            seen = seen + here
+        return seen, place, place_col
+
+    seen, place, place_col = locate(c, r)
+    for copy in loads:
+        copy.wait()
     tiles = []
     partial = [jnp.zeros((1, TILE), jnp.float32) for _ in range(tc)]
     for s in range(SLOTS):
         tile = jnp.where(seen > s, values[place[s]], 0.0)
         tiles.append(tile)
+        raw_own[s] = tile
         total = jnp.sum(tile, axis=0, keepdims=True)
         for j in range(tc):
             partial[j] = partial[j] + jnp.where(place_col[s] == j, total, 0.0)
@@ -127,69 +148,17 @@
     def drain(parts_ref, send_sem):
         pltpu.make_async_copy(parts_ref, parts_ref, send_sem).wait()
 
+    other = 1 - zh
+    partner = col_of(other, y, core)
     exchange(in_own, in_parts, in_send, in_recv)
-    in_sum = collect(in_own, in_parts, in_recv)
-    for j in range(tc):
-        in_total[j] = in_sum[:, j * TILE : (j + 1) * TILE]
-    for s in range(SLOTS):
-        stoch = (tiles[s] / in_total[place_col[s]]).astype(jnp.bfloat16)
-        a_pack[SLOTS * r + s] = stoch
-        b_pack[SLOTS * c + s] = stoch
-    b_pack[SLOTS * cols] = jnp.zeros((TILE, TILE), jnp.bfloat16)
-
-    a_count, b_count = 0, 0
-
-    def packed(ref, origin):
-        return ref.at[pl.ds(SLOTS * origin, SLOTS)]
-
-    def arrived(ref, origin, sem):
-        pltpu.make_async_copy(packed(ref, origin), packed(ref, origin), sem).wait()
-
-    def send_a(origin, peer):
-        nonlocal a_count
-        pltpu.make_async_remote_copy(
-            src_ref=packed(a_pack, origin),
-            dst_ref=packed(a_pack, origin),
-            send_sem=a_send.at[a_count],
-            recv_sem=a_recv.at[origin],
-            device_id={"row": peer},
-        ).start()
-        a_count += 1
-
-    def send_b(origin, peer):
-        nonlocal b_count
-        pltpu.make_async_remote_copy(
-            src_ref=packed(b_pack, origin),
-            dst_ref=packed(b_pack, origin),
-            send_sem=b_send.at[b_count],
-            recv_sem=b_recv.at[origin],
-            device_id={"col": peer},
-        ).start()
-        b_count += 1
-
-    def wait_a(origin):
-        arrived(a_pack, origin, a_recv.at[origin])
-
-    def wait_b(origin):
-        arrived(b_pack, origin, b_recv.at[origin])
-
-    sibling = col_of(zh, y, 1 - core)
-    up = col_of(zh, (y + 1) % y_size, core)
-    down = col_of(zh, (y + y_size - 1) % y_size, core)
-    other = 1 - zh
-    half = y_size // 2
-
-    def around_x(origin):
-        for d in (1, x_size - 1, *range(2, x_size - 1)):
-            send_a(origin, row_of(zl, (x + d) % x_size))
-
-    send_b(c, up)
-    send_b(c, down)
-    around_x(r)
-    send_b(c, col_of(other, y, core))
-    for d in range(1, Z_LO):
-        send_a(r, row_of((zl + d) % Z_LO, x))
-    send_b(c, sibling)
+    raw_copy = pltpu.make_async_remote_copy(
+        src_ref=raw_own,
+        dst_ref=raw_other,
+        send_sem=raw_sem.at[0],
+        recv_sem=raw_sem.at[1],
+        device_id={"col": partner},
+    )
+    raw_copy.start()
 
     def locate_b(block, carry):
         count = jnp.int32(0)
@@ -219,30 +188,130 @@
 
     lax.fori_loop(0, rows, locate_a, 0)
 
-    def pass_on(origin, peer, last):
-        wait_b(origin)
-        if not last:
-            send_b(origin, peer)
+    _, _, other_col = locate(partner, r)
+    in_sum = collect(in_own, in_parts, in_recv)
+    for j in range(tc):
+        in_total[j] = in_sum[:, j * TILE : (j + 1) * TILE]
+    for s in range(SLOTS):
+        stoch = (tiles[s] / in_total[place_col[s]]).astype(jnp.bfloat16)
+        a_pack[SLOTS * r + s] = stoch
+        b_pack[SLOTS * c + s] = stoch
+    b_pack[SLOTS * cols] = jnp.zeros((TILE, TILE), jnp.bfloat16)
+
+    a_count, b_count = 0, 0
+
+    def packed(ref, origin):
+        return ref.at[pl.ds(SLOTS * origin, SLOTS)]
+
+    def arrived(ref, origin, sem):
+        pltpu.make_async_copy(packed(ref, origin), packed(ref, origin), sem).wait()
+
+    def send_a(origin, peer):
+        nonlocal a_count
+        pltpu.make_async_remote_copy(
+            src_ref=packed(a_pack, origin),
+            dst_ref=packed(a_pack, origin),
+            send_sem=a_send.at[a_count],
+            recv_sem=a_recv.at[origin],
+            device_id={"row": peer},
+        ).start()
+        a_count += 1
+
+    def send_b(origin, peer):
+        nonlocal b_count
+        pltpu.make_async_remote_copy(
+            src_ref=packed(b_pack, origin),
+            dst_ref=packed(b_pack, origin),
+            send_sem=b_send.at[b_count],
+            recv_sem=b_recv.at[origin],
+            device_id={"col": peer},
+        ).start()
+        b_count += 1
+
+    def wait_a(origin):
+        arrived(a_pack, origin, a_recv.at[origin])
+
+    def wait_b(origin):
+        arrived(b_pack, origin, b_recv.at[origin])
+
+    sibling = col_of(zh, y, 1 - core)
+    half = y_size // 2
+
+    def y_at(zh_, d):
+        return col_of(zh_, (y + d + y_size) % y_size, core)
+
+    def around_x(origin):
+        for d in (1, x_size - 1, *range(2, x_size - 1)):
+            send_a(origin, row_of(zl, (x + d) % x_size))
+
+    def around_y(origin):
+        for d in (1, -1, 2, -2):
+            send_b(origin, y_at(zh, d))
         send_b(origin, sibling)
 
-    for step in range(1, half + 1):
-        pass_on(col_of(zh, (y + y_size - step) % y_size, core), up, step == half)
-        if step < half:
-            pass_on(col_of(zh, (y + step) % y_size, core), down, step == half - 1)
-        if step < Z_LO:
-            origin = row_of((zl + step) % Z_LO, x)
-            wait_a(origin)
-            around_x(origin)
-        if step == 1:
-            origin = col_of(other, y, core)
-            wait_b(origin)
-            send_b(origin, up)
-            send_b(origin, down)
-            send_b(origin, sibling)
-        else:
-            pass_on(col_of(other, (y + y_size - step + 1) % y_size, core), up, step == half)
-            pass_on(col_of(other, (y + step - 1) % y_size, core), down, False)
-    pass_on(col_of(other, (y + half) % y_size, core), down, True)
+    def send_far(origin, s, sign):
+        nonlocal far_count
+        tile = b_pack.at[SLOTS * origin + s]
+        pltpu.make_async_remote_copy(
+            src_ref=tile,
+            dst_ref=tile,
+            send_sem=far_send.at[far_count],
+            recv_sem=far_recv.at[far_count],
+            device_id={"col": y_at(zh, sign)},
+        ).start()
+        far_count += 1
+
+    def near(zh_, d):
+        wait_b(y_at(zh_, d))
+        send_b(y_at(zh_, d), sibling)
+
+    def forward(zh_, d):
+        wait_b(y_at(zh_, d))
+        send_b(y_at(zh_, d), y_at(zh, -1 if d > 0 else 1))
+        send_b(y_at(zh_, d), sibling)
+
+    def forward_far(zh_, d):
+        wait_b(y_at(zh_, d))
+        send_far(y_at(zh_, d), 0 if d > 0 else 1, -1 if d > 0 else 1)
+        send_b(y_at(zh_, d), sibling)
+
+    def z_arrival(d):
+        origin = row_of((zl + d) % Z_LO, x)
+        wait_a(origin)
+        around_x(origin)
+
+    far_count = 0
+    around_y(c)
+    for d in (1, 3, 2):
+        send_a(r, row_of((zl + d) % Z_LO, x))
+    around_x(r)
+    raw_copy.wait_recv()
+    for s in range(SLOTS):
+        stoch = (raw_other[s] / in_total[other_col[s]]).astype(jnp.bfloat16)
+        b_pack[SLOTS * partner + s] = stoch
+    around_y(partner)
+
+    near(zh, 1)
+    near(zh, -1)
+    z_arrival(1)
+    z_arrival(3)
+    forward(zh, 2)
+    forward(zh, -2)
+    z_arrival(2)
+    near(other, 1)
+    near(other, -1)
+    forward(other, 2)
+    forward(other, -2)
+    forward_far(zh, 3)
+    forward_far(zh, -3)
+    forward_far(other, 3)
+    forward_far(other, -3)
+    for n, zh_ in ((0, zh), (2, other)):
+        origin = y_at(zh_, half)
+        for s in range(SLOTS):
+            tile = b_pack.at[SLOTS * origin + s]
+            pltpu.make_async_copy(tile, tile, far_recv.at[n + s]).wait()
+        send_b(origin, sibling)
 
     for zl_ in range(Z_LO):
         for d in range(1, x_size):
@@ -275,7 +344,7 @@
         )
         return carry
 
-    lax.fori_loop(0, rows, multiply, 0)
+    lax.fori_loop(0, rows, multiply, 0, unroll=4)
 
     sums = []
     for j in range(tc):
@@ -290,18 +359,24 @@
     out_own[...] = jnp.concatenate(sums, axis=1)
 
     exchange(out_own, out_parts, out_send, out_recv)
+    store = pltpu.make_async_copy(result, result_hbm, store_sem.at[0])
+    store.start()
+    raw_copy.wait_send()
     drain(in_parts, in_send)
     for n in range(a_count):
         arrived(a_pack, 0, a_send.at[n])
     for n in range(b_count):
         arrived(b_pack, 0, b_send.at[n])
+    for n in range(far_count):
+        pltpu.make_async_copy(b_pack.at[0], b_pack.at[0], far_send.at[n]).wait()
     out_sum = collect(out_own, out_parts, out_recv)
     order = tr * TILE * cols
-    result[...] = result[...] * (order / out_sum)
-    store = pltpu.make_async_copy(result, out_hbm, store_sem)
-    store.start()
+    scale[...] = order / out_sum
+    store_scale = pltpu.make_async_copy(scale, scale_hbm, store_sem.at[1])
+    store_scale.start()
     drain(out_parts, out_send)
     store.wait()
+    store_scale.wait()
 
 
 def on_device(rows, cols, values, pattern, prune):
@@ -309,17 +384,21 @@
     height, width = values.shape
     f32, bf16 = jnp.float32, jnp.bfloat16
     dma = pltpu.SemaphoreType.DMA
-    return pl.pallas_call(
+    inflated, scale = pl.pallas_call(
         functools.partial(kernel, rows, cols),
-        out_shape=jax.ShapeDtypeStruct((height, width), f32),
-        in_specs=[
-            pl.BlockSpec(memory_space=pl.ANY),
-            pl.BlockSpec(memory_space=pltpu.SMEM),
-            pl.BlockSpec(memory_space=pltpu.SMEM),
+        out_shape=[
+            jax.ShapeDtypeStruct((height, width), f32),
+            jax.ShapeDtypeStruct((1, width), f32),
         ],
-        out_specs=pl.BlockSpec(memory_space=pl.ANY),
+        in_specs=[pl.BlockSpec(memory_space=pl.ANY)] * 3,
+        out_specs=[pl.BlockSpec(memory_space=pl.ANY)] * 2,
         scratch_shapes=[
             pltpu.VMEM((tr * tc, TILE, TILE), f32),
+            pltpu.SMEM(pattern.shape, jnp.int32),
+            pltpu.SMEM(prune.shape, jnp.int32),
+            pltpu.VMEM((SLOTS, TILE, TILE), f32),
+            pltpu.VMEM((SLOTS, TILE, TILE), f32),
+            pltpu.VMEM((1, width), f32),
             pltpu.VMEM((rows * SLOTS, TILE, TILE), bf16),
             pltpu.VMEM((cols * SLOTS + 1, TILE, TILE), bf16),
             pltpu.VMEM((1, width), f32),
@@ -332,7 +411,11 @@
             pltpu.SMEM((rows * SLOTS,), jnp.int32),
             pltpu.SMEM((rows * SLOTS,), jnp.int32),
             dma((tr * tc,)),
-            dma,
+            dma((2,)),
+            dma((2,)),
+            dma((2,)),
+            dma((4,)),
+            dma((4,)),
             dma,
             dma,
             dma,
@@ -345,7 +428,7 @@
         compiler_params=pltpu.CompilerParams(
             collective_id=0,
             has_side_effects=True,
-            vmem_limit_bytes=32 * 1024 * 1024,
+            vmem_limit_bytes=60 * 1024 * 1024,
         ),
         cost_estimate=pl.CostEstimate(
             flops=2 * height * width * TILE * SLOTS * rows,
@@ -353,6 +436,7 @@
             transcendentals=0,
         ),
     )(values, pattern, prune)
+    return inflated * scale
 
 
 def solution(mesh):

time: 64.2 us -> 57.3 us (0.89)
  Pallas kernels: 60.4 us -> 54.4 us
  local copies, waits for them, and re-layouts: 3.27 us -> 0.66 us
  other arithmetic: 0 us -> 1.9 us
    pallas_call x1, Pallas kernels: 60.4 us -> 54.4 us  [on_device(): pl.pallas_call(functools.partial(kernel, rows, cols), out_shape=[jax.Shap...]
    unnamed x7 -> x2, local copies, waits for them, and re-layouts: 3.27 us -> 0.66 us
    mul x0 -> x1, other arithmetic: none -> 1.9 us  [on_device(): return inflated * scale]
where the time goes in v2:
time: 57.3 us; the launch traced here: 57 us
  Pallas kernels  54.4 us (95%)
  other arithmetic  1.9 us (3%)
  local copies, waits for them, and re-layouts  0.66 us (1%)
    pallas_call x1, Pallas kernels, on_device(): pl.pallas_call(functools.partial(kernel, rows, cols), out_shape=[jax.Shap...  54.4 us
    mul x1, other arithmetic, on_device(): return inflated * scale  1.9 us

profile of v2, /device:TPU:1, one launch (start us, length us, event | category | flops | bytes accessed | tf_op | source)
XLA Modules:
  0.0 57.0 jit_solution(1099776182159505038)
XLA Ops:
  0.0 54.4 %shard_map.37 = (f32[256,512]{1,0:T(8,128)}, f32[1,512]{1,0:T(1,128)}) custom-call(f32[256,512]{1,0:T(8,128)} %values_hbm.1, s32[64,64]{1,0:T(8,128)} %pattern_hbm.1, s32[2,4]{1,0:T(2,128)} %prune_hbm.1), custom_call_target="tpu_custom_call" | custom-call | flops 1073741824 | bytes 1048576 | tf_op jit(solution)/shard_map/pallas_call | solution.py:387
  54.4 0.0 copy-start
  54.5 0.7 %copy-done = f32[1,512]{1,0:T(1,128)S(1)} copy-done((f32[1,512]{1,0:T(1,128)S(1)}, f32[1,512]{1,0:T(1,128)}, u32[]{:S(2)}) %copy-start) | copy-done | bytes 2072
  55.1 1.9 %broadcast_multiply_fusion = f32[256,512]{1,0:T(8,128)} fusion(f32[256,512]{1,0:T(8,128)} %get-tuple-element.7, f32[512]{0:T(512)S(1)} %bitcast.1), kind=kLoop, calls=%fused_computation | loop fusion | flops 131072 | bytes 1050624 | tf_op jit(solution)/shard_map/mul | solution.py:439
Async XLA Ops:
  54.4 0.7 %copy-start = (f32[1,512]{1,0:T(1,128)S(1)}, f32[1,512]{1,0:T(1,128)}, u32[]{:S(2)}) copy-start(f32[1,512]{1,0:T(1,128)} %get-tuple-element.8) | copy-start | bytes 6148

commit v3 on v2

--- a/solution.py
+++ b/solution.py
@@ -26,7 +26,9 @@
     pattern,
     prune,
     raw_own,
-    raw_other,
+    raw_in,
+    pair_part,
+    in_pair,
     scale,
     a_pack,
     b_pack,
@@ -42,7 +44,9 @@
     load_sem,
     store_sem,
     fetch_sem,
-    raw_sem,
+    raw_send,
+    raw_recv,
+    pair_sem,
     far_send,
     far_recv,
     in_send,
@@ -86,16 +90,30 @@
 
     barrier = pltpu.get_barrier_semaphore()
 
-    def greet_col(d, carry):
-        pl.semaphore_signal(barrier, inc=1, device_id={"col": (c + d) % cols})
-        return carry
-
-    lax.fori_loop(1, cols, greet_col, 0)
+    other = 1 - zh
+    partner = col_of(other, y, core)
+
+    def y_at(zh_, d):
+        return col_of(zh_, (y + d + y_size) % y_size, core)
+
+    def ring(d):
+        return min(d, y_size - d)
+
+    offsets = [(dz, dy, dc) for dz in range(Z_HI) for dy in range(y_size) for dc in range(CORES)]
+    offsets.sort(key=lambda o: -(Z_LO * o[0] + ring(o[1])))
+    offsets.remove((0, 0, 0))
+
+    def at_offset(dz, dy, dc):
+        return col_of((zh + dz) % Z_HI, (y + dy) % y_size, (core + dc) % CORES)
+
+    all_peers = [at_offset(*o) for o in offsets]
+    half_peers = [at_offset(*o) for o in offsets if o[0] == 0]
     row_peers = [row_of((zl + d) % Z_LO, x) for d in range(1, Z_LO)]
     row_peers += [row_of(zl, (x + d) % x_size) for d in range(1, x_size)]
+    for peer in [partner, *half_peers]:
+        pl.semaphore_signal(barrier, inc=1, device_id={"col": peer})
     for peer in row_peers:
         pl.semaphore_signal(barrier, inc=1, device_id={"row": peer})
-
     for copy in fetches:
         copy.wait()
 
@@ -126,20 +144,17 @@
             partial[j] = partial[j] + jnp.where(place_col[s] == j, total, 0.0)
     in_own[...] = jnp.concatenate(partial, axis=1)
 
-    pl.semaphore_wait(barrier, cols - 1 + len(row_peers))
-
-    def exchange(own_ref, parts_ref, send_sem, recv_sem):
-        def send(d, carry):
+    pl.semaphore_wait(barrier, 1 + len(half_peers) + len(row_peers))
+
+    def exchange(peers, own_ref, parts_ref, send_sem, recv_sem):
+        for n, peer in enumerate(peers):
             pltpu.make_async_remote_copy(
                 src_ref=own_ref,
-                dst_ref=parts_ref.at[cols - 1 - d],
+                dst_ref=parts_ref.at[n],
                 send_sem=send_sem,
                 recv_sem=recv_sem,
-                device_id={"col": (c + d) % cols},
+                device_id={"col": peer},
             ).start()
-            return carry
-
-        lax.fori_loop(1, cols, send, 0)
 
     def collect(own_ref, parts_ref, recv_sem):
         pltpu.make_async_copy(parts_ref, parts_ref, recv_sem).wait()
@@ -148,17 +163,27 @@
     def drain(parts_ref, send_sem):
         pltpu.make_async_copy(parts_ref, parts_ref, send_sem).wait()
 
-    other = 1 - zh
-    partner = col_of(other, y, core)
-    exchange(in_own, in_parts, in_send, in_recv)
-    raw_copy = pltpu.make_async_remote_copy(
-        src_ref=raw_own,
-        dst_ref=raw_other,
-        send_sem=raw_sem.at[0],
-        recv_sem=raw_sem.at[1],
-        device_id={"col": partner},
-    )
-    raw_copy.start()
+    exchange([partner], in_own, pair_part, pair_sem.at[0], pair_sem.at[1])
+    reach = (2, -2, 1, -1)
+    raw_reach = (2, -2)
+    raw_sends = []
+
+    def send_raw(peer, slot):
+        copy = pltpu.make_async_remote_copy(
+            src_ref=raw_own,
+            dst_ref=raw_in.at[slot],
+            send_sem=raw_send.at[slot],
+            recv_sem=raw_recv.at[slot],
+            device_id={"col": peer},
+        )
+        copy.start()
+        raw_sends.append(copy)
+
+    send_raw(partner, 0)
+    in_pair[...] = collect(in_own, pair_part, pair_sem.at[1])
+    exchange(half_peers, in_pair, in_parts, in_send, in_recv)
+    for d in raw_reach:
+        send_raw(y_at(zh, d), 1 + reach.index(-d))
 
     def locate_b(block, carry):
         count = jnp.int32(0)
@@ -188,8 +213,9 @@
 
     lax.fori_loop(0, rows, locate_a, 0)
 
-    _, _, other_col = locate(partner, r)
-    in_sum = collect(in_own, in_parts, in_recv)
+    raw_origins = [partner, *(y_at(zh, d) for d in reach)]
+    raw_cols = [locate(origin, r)[2] for origin in raw_origins]
+    in_sum = collect(in_pair, in_parts, in_recv)
     for j in range(tc):
         in_total[j] = in_sum[:, j * TILE : (j + 1) * TILE]
     for s in range(SLOTS):
@@ -206,13 +232,13 @@
     def arrived(ref, origin, sem):
         pltpu.make_async_copy(packed(ref, origin), packed(ref, origin), sem).wait()
 
-    def send_a(origin, peer):
+    def send_a(origin, s, peer):
         nonlocal a_count
         pltpu.make_async_remote_copy(
-            src_ref=packed(a_pack, origin),
-            dst_ref=packed(a_pack, origin),
+            src_ref=a_pack.at[SLOTS * origin + s],
+            dst_ref=a_pack.at[SLOTS * origin + s],
             send_sem=a_send.at[a_count],
-            recv_sem=a_recv.at[origin],
+            recv_sem=a_recv.at[SLOTS * origin + s],
             device_id={"row": peer},
         ).start()
         a_count += 1
@@ -228,8 +254,9 @@
         ).start()
         b_count += 1
 
-    def wait_a(origin):
-        arrived(a_pack, origin, a_recv.at[origin])
+    def wait_a(origin, s):
+        tile = a_pack.at[SLOTS * origin + s]
+        pltpu.make_async_copy(tile, tile, a_recv.at[SLOTS * origin + s]).wait()
 
     def wait_b(origin):
         arrived(b_pack, origin, b_recv.at[origin])
@@ -237,19 +264,13 @@
     sibling = col_of(zh, y, 1 - core)
     half = y_size // 2
 
-    def y_at(zh_, d):
-        return col_of(zh_, (y + d + y_size) % y_size, core)
-
-    def around_x(origin):
-        for d in (1, x_size - 1, *range(2, x_size - 1)):
-            send_a(origin, row_of(zl, (x + d) % x_size))
-
-    def around_y(origin):
-        for d in (1, -1, 2, -2):
-            send_b(origin, y_at(zh, d))
-        send_b(origin, sibling)
-
-    def send_far(origin, s, sign):
+    def around_x(origin, s):
+        for d in (*range(2, x_size - 1), 1, x_size - 1):
+            send_a(origin, s, row_of(zl, (x + d) % x_size))
+
+    far_count = 0
+
+    def send_far(origin, s, d):
         nonlocal far_count
         tile = b_pack.at[SLOTS * origin + s]
         pltpu.make_async_remote_copy(
@@ -257,55 +278,66 @@
             dst_ref=tile,
             send_sem=far_send.at[far_count],
             recv_sem=far_recv.at[far_count],
-            device_id={"col": y_at(zh, sign)},
+            device_id={"col": y_at(zh, d)},
         ).start()
         far_count += 1
 
-    def near(zh_, d):
+    def raw_arrival(n):
+        origin = raw_origins[n]
+        pltpu.make_async_copy(raw_in.at[n], raw_in.at[n], raw_recv.at[n]).wait()
+        for s in range(SLOTS):
+            stoch = (raw_in[n, s] / in_total[raw_cols[n][s]]).astype(jnp.bfloat16)
+            b_pack[SLOTS * origin + s] = stoch
+
+    def spread(zh_, d):
+        sign = -1 if d > 0 else 1
+        send_far(y_at(zh_, d), 0 if d > 0 else 1, 2 * sign)
+        send_b(y_at(zh_, d), y_at(zh, sign))
+        send_b(y_at(zh_, d), sibling)
+
+    def arrive(zh_, d):
         wait_b(y_at(zh_, d))
         send_b(y_at(zh_, d), sibling)
 
-    def forward(zh_, d):
-        wait_b(y_at(zh_, d))
-        send_b(y_at(zh_, d), y_at(zh, -1 if d > 0 else 1))
-        send_b(y_at(zh_, d), sibling)
-
-    def forward_far(zh_, d):
-        wait_b(y_at(zh_, d))
-        send_far(y_at(zh_, d), 0 if d > 0 else 1, -1 if d > 0 else 1)
-        send_b(y_at(zh_, d), sibling)
-
-    def z_arrival(d):
+    def z_arrival(d, s):
         origin = row_of((zl + d) % Z_LO, x)
-        wait_a(origin)
-        around_x(origin)
-
-    far_count = 0
-    around_y(c)
-    for d in (1, 3, 2):
-        send_a(r, row_of((zl + d) % Z_LO, x))
-    around_x(r)
-    raw_copy.wait_recv()
+        wait_a(origin, s)
+        around_x(origin, s)
+
+    for d in reach:
+        if d not in raw_reach:
+            send_b(c, y_at(zh, d))
     for s in range(SLOTS):
-        stoch = (raw_other[s] / in_total[other_col[s]]).astype(jnp.bfloat16)
-        b_pack[SLOTS * partner + s] = stoch
-    around_y(partner)
-
-    near(zh, 1)
-    near(zh, -1)
-    z_arrival(1)
-    z_arrival(3)
-    forward(zh, 2)
-    forward(zh, -2)
-    z_arrival(2)
-    near(other, 1)
-    near(other, -1)
-    forward(other, 2)
-    forward(other, -2)
-    forward_far(zh, 3)
-    forward_far(zh, -3)
-    forward_far(other, 3)
-    forward_far(other, -3)
+        for d in (2, 1, 3):
+            send_a(r, s, row_of((zl + d) % Z_LO, x))
+    for s in range(SLOTS):
+        around_x(r, s)
+    send_b(c, sibling)
+    raw_arrival(0)
+    for d in reach:
+        send_b(partner, y_at(zh, d))
+    send_b(partner, sibling)
+    for n, d in enumerate(reach, 1):
+        if d in raw_reach:
+            raw_arrival(n)
+            if abs(d) == 2:
+                spread(zh, d)
+            else:
+                send_b(raw_origins[n], sibling)
+    for s in range(SLOTS):
+        for d in (1, 3, 2):
+            z_arrival(d, s)
+    for zh_ in (zh, other):
+        for d in reach:
+            if zh_ is zh and d in raw_reach:
+                continue
+            wait_b(y_at(zh_, d))
+            if abs(d) == 2:
+                spread(zh_, d)
+            else:
+                send_b(y_at(zh_, d), sibling)
+    for zh_, d in ((zh, 3), (zh, -3), (other, 3), (other, -3)):
+        arrive(zh_, d)
     for n, zh_ in ((0, zh), (2, other)):
         origin = y_at(zh_, half)
         for s in range(SLOTS):
@@ -315,7 +347,8 @@
 
     for zl_ in range(Z_LO):
         for d in range(1, x_size):
-            wait_a(row_of((zl + zl_) % Z_LO, (x + d) % x_size))
+            for s in range(SLOTS):
+                wait_a(row_of((zl + zl_) % Z_LO, (x + d) % x_size), s)
 
     def wait_sibling(block, carry):
         wait_b(block * CORES + 1 - core)
@@ -358,13 +391,15 @@
         sums.append(col_sum)
     out_own[...] = jnp.concatenate(sums, axis=1)
 
-    exchange(out_own, out_parts, out_send, out_recv)
+    exchange(all_peers, out_own, out_parts, out_send, out_recv)
     store = pltpu.make_async_copy(result, result_hbm, store_sem.at[0])
     store.start()
-    raw_copy.wait_send()
+    drain(pair_part, pair_sem.at[0])
+    for copy in raw_sends:
+        copy.wait_send()
     drain(in_parts, in_send)
     for n in range(a_count):
-        arrived(a_pack, 0, a_send.at[n])
+        pltpu.make_async_copy(a_pack.at[0], a_pack.at[0], a_send.at[n]).wait()
     for n in range(b_count):
         arrived(b_pack, 0, b_send.at[n])
     for n in range(far_count):
@@ -390,19 +425,21 @@
             jax.ShapeDtypeStruct((height, width), f32),
             jax.ShapeDtypeStruct((1, width), f32),
         ],
-        in_specs=[pl.BlockSpec(memory_space=pl.ANY)] * 3,
+        in_specs=[pl.BlockSpec(memory_space=pltpu.HBM)] * 3,
         out_specs=[pl.BlockSpec(memory_space=pl.ANY)] * 2,
         scratch_shapes=[
             pltpu.VMEM((tr * tc, TILE, TILE), f32),
             pltpu.SMEM(pattern.shape, jnp.int32),
             pltpu.SMEM(prune.shape, jnp.int32),
             pltpu.VMEM((SLOTS, TILE, TILE), f32),
-            pltpu.VMEM((SLOTS, TILE, TILE), f32),
+            pltpu.VMEM((5, SLOTS, TILE, TILE), f32),
+            pltpu.VMEM((1, 1, width), f32),
+            pltpu.VMEM((1, width), f32),
             pltpu.VMEM((1, width), f32),
             pltpu.VMEM((rows * SLOTS, TILE, TILE), bf16),
             pltpu.VMEM((cols * SLOTS + 1, TILE, TILE), bf16),
             pltpu.VMEM((1, width), f32),
-            pltpu.VMEM((cols - 1, 1, width), f32),
+            pltpu.VMEM((cols // Z_HI - 1, 1, width), f32),
             pltpu.VMEM((tc, 1, TILE), f32),
             pltpu.VMEM((1, width), f32),
             pltpu.VMEM((cols - 1, 1, width), f32),
@@ -413,6 +450,8 @@
             dma((tr * tc,)),
             dma((2,)),
             dma((2,)),
+            dma((5,)),
+            dma((5,)),
             dma((2,)),
             dma((4,)),
             dma((4,)),
@@ -420,22 +459,22 @@
             dma,
             dma,
             dma,
-            dma((rows,)),
-            dma((rows,)),
+            dma((rows * SLOTS,)),
+            dma((rows * SLOTS,)),
             dma((cols,)),
             dma((cols,)),
         ],
         compiler_params=pltpu.CompilerParams(
             collective_id=0,
             has_side_effects=True,
-            vmem_limit_bytes=60 * 1024 * 1024,
+            vmem_limit_bytes=32 * 1024 * 1024,
         ),
         cost_estimate=pl.CostEstimate(
             flops=2 * height * width * TILE * SLOTS * rows,
             bytes_accessed=2 * 4 * height * width,
             transcendentals=0,
         ),
-    )(values, pattern, prune)
+    )(*(pltpu.with_memory_space_constraint(x, pltpu.HBM) for x in (values, pattern, prune)))
     return inflated * scale
 
 

time: 57.3 us -> 51.3 us (0.90); the launches traced: 57 us -> 50.4 us
  Pallas kernels: 54.4 us -> 49.5 us
  other arithmetic: 1.9 us -> 0.86 us
  local copies, waits for them, and re-layouts: 0.66 us -> 0 us
    pallas_call x1, Pallas kernels: 54.4 us -> 49.5 us  [on_device(): pl.pallas_call(functools.partial(kernel, rows, cols), out_shape=[jax.Shap...]
    mul x1, other arithmetic: 1.9 us -> 0.86 us  [on_device(): return inflated * scale]
    unnamed x2 -> x0, local copies, waits for them, and re-layouts: 0.66 us -> none
where the time goes in v3:
time: 51.3 us; the launch traced here: 50.4 us
  Pallas kernels  49.5 us (96%)
  other arithmetic  0.86 us (2%)
    pallas_call x1, Pallas kernels, on_device(): pl.pallas_call(functools.partial(kernel, rows, cols), out_shape=[jax.Shap...  49.5 us

profile of v3, /device:TPU:1, one launch (start us, length us, event | category | flops | bytes accessed | tf_op | source)
XLA Modules:
  0.0 50.4 jit_solution(1390429472293833050)
XLA Ops:
  0.0 49.5 %shard_map.37 = (f32[256,512]{1,0:T(8,128)S(1)}, f32[1,512]{1,0:T(1,128)S(1)}) custom-call(f32[256,512]{1,0:T(8,128)} %values_hbm.1, s32[64,64]{1,0:T(8,128)} %pattern_hbm.1, s32[2,4]{1,0:T(2,128)} %prune_hbm.1), custom_call_target="tpu_custom_call" | custom-call | flops 1073741824 | bytes 1048576 | tf_op jit(solution)/shard_map/pallas_call | solution.py:422
  49.5 0.9 %broadcast_multiply_fusion = f32[256,512]{1,0:T(8,128)} fusion(f32[256,512]{1,0:T(8,128)S(1)} %get-tuple-element.7, f32[512]{0:T(512)S(1)} %bitcast.1), kind=kLoop, calls=%fused_computation | loop fusion | flops 131072 | bytes 1050624 | tf_op jit(solution)/shard_map/mul | solution.py:478

commit v4 on v3

--- a/solution.py
+++ b/solution.py
@@ -28,6 +28,7 @@
     raw_own,
     raw_in,
     pair_part,
+    cross_parts,
     in_pair,
     scale,
     a_pack,
@@ -47,6 +48,11 @@
     raw_send,
     raw_recv,
     pair_sem,
+    cross_send,
+    cross_recv,
+    partner_here,
+    half_here,
+    row_here,
     far_send,
     far_recv,
     in_send,
@@ -73,6 +79,66 @@
     def col_of(zh_, y_, core_):
         return (zh_ * y_size + y_) * CORES + core_
 
+    other = 1 - zh
+    partner = col_of(other, y, core)
+
+    def y_at(zh_, d):
+        return col_of(zh_, (y + d + y_size) % y_size, core)
+
+    def ring(d):
+        return min(d, y_size - d)
+
+    offsets = [(dz, dy, dc) for dz in range(Z_HI) for dy in range(y_size) for dc in range(CORES)]
+    offsets.sort(key=lambda o: -(Z_LO * o[0] + ring(o[1])))
+    offsets.remove((0, 0, 0))
+
+    def at_offset(dz, dy, dc):
+        return col_of((zh + dz) % Z_HI, (y + dy) % y_size, (core + dc) % CORES)
+
+    all_peers = [at_offset(*o) for o in offsets]
+    half_peers = [at_offset(*o) for o in offsets if o[0] == 0]
+    other_half = [at_offset(*o) for o in offsets if o[0] == 1]
+
+    late_first = (rows - 1 - r) // (rows - 1) * (1 - zh)
+
+    def rank_of(y_, core_):
+        side = (y_ + y_size // 2 - 1) // y_size
+        first = (y_size - 1 - y_) // (y_size - 1)
+        place = ((1 - side) * (2 * y_ - 1) + side * 2 * (y_size - y_) + first) * CORES + core_
+        return (place - late_first + cols // Z_HI) % (cols // Z_HI)
+
+    rank = rank_of(y, core)
+    half_ranks = [rank_of((y + dy) % y_size, (core + dc) % CORES) for dz, dy, dc in offsets if dz == 0]
+    row_peers = [row_of((zl + d) % Z_LO, x) for d in (3, 2, 1)]
+    row_peers += [row_of(zl, (x + d) % x_size) for d in range(1, x_size)]
+    barrier = pltpu.get_barrier_semaphore()
+
+    def await_some(sem, count):
+        pl.when(count > 0)(lambda: pl.semaphore_wait(sem, count))
+
+    def signal(sem, axis, peer):
+        pl.semaphore_signal(sem, inc=1, device_id={axis: peer})
+
+    @pl.when(zh == 0)
+    def _():
+        for peer in other_half:
+            signal(barrier, "col", peer)
+
+    for peer, peer_rank in zip(half_peers, half_ranks, strict=True):
+        pl.when(peer_rank > rank)(functools.partial(signal, barrier, "col", peer))
+    for peer in row_peers:
+        pl.when(peer > r)(functools.partial(signal, barrier, "row", peer))
+    await_some(barrier, rank + zl + x + zh * (cols // Z_HI))
+
+    @pl.when(zh == 1)
+    def _():
+        signal(partner_here, "col", partner)
+
+    for peer, peer_rank in zip(half_peers, half_ranks, strict=True):
+        pl.when(peer_rank < rank)(functools.partial(signal, half_here, "col", peer))
+    for peer in row_peers:
+        pl.when(peer < r)(functools.partial(signal, row_here, "row", peer))
+
     loads = [
         pltpu.make_async_copy(
             values_hbm.at[pl.ds(t // tc * TILE, TILE), pl.ds(t % tc * TILE, TILE)],
@@ -88,32 +154,6 @@
     for copy in fetches + loads:
         copy.start()
 
-    barrier = pltpu.get_barrier_semaphore()
-
-    other = 1 - zh
-    partner = col_of(other, y, core)
-
-    def y_at(zh_, d):
-        return col_of(zh_, (y + d + y_size) % y_size, core)
-
-    def ring(d):
-        return min(d, y_size - d)
-
-    offsets = [(dz, dy, dc) for dz in range(Z_HI) for dy in range(y_size) for dc in range(CORES)]
-    offsets.sort(key=lambda o: -(Z_LO * o[0] + ring(o[1])))
-    offsets.remove((0, 0, 0))
-
-    def at_offset(dz, dy, dc):
-        return col_of((zh + dz) % Z_HI, (y + dy) % y_size, (core + dc) % CORES)
-
-    all_peers = [at_offset(*o) for o in offsets]
-    half_peers = [at_offset(*o) for o in offsets if o[0] == 0]
-    row_peers = [row_of((zl + d) % Z_LO, x) for d in range(1, Z_LO)]
-    row_peers += [row_of(zl, (x + d) % x_size) for d in range(1, x_size)]
-    for peer in [partner, *half_peers]:
-        pl.semaphore_signal(barrier, inc=1, device_id={"col": peer})
-    for peer in row_peers:
-        pl.semaphore_signal(barrier, inc=1, device_id={"row": peer})
     for copy in fetches:
         copy.wait()
 
@@ -144,8 +184,6 @@
             partial[j] = partial[j] + jnp.where(place_col[s] == j, total, 0.0)
     in_own[...] = jnp.concatenate(partial, axis=1)
 
-    pl.semaphore_wait(barrier, 1 + len(half_peers) + len(row_peers))
-
     def exchange(peers, own_ref, parts_ref, send_sem, recv_sem):
         for n, peer in enumerate(peers):
             pltpu.make_async_remote_copy(
@@ -163,27 +201,31 @@
     def drain(parts_ref, send_sem):
         pltpu.make_async_copy(parts_ref, parts_ref, send_sem).wait()
 
-    exchange([partner], in_own, pair_part, pair_sem.at[0], pair_sem.at[1])
     reach = (2, -2, 1, -1)
     raw_reach = (2, -2)
-    raw_sends = []
-
-    def send_raw(peer, slot):
-        copy = pltpu.make_async_remote_copy(
+    raw_origins = [partner, *(y_at(zh, d) for d in raw_reach)]
+
+    def raw_copy(peer, slot):
+        return pltpu.make_async_remote_copy(
             src_ref=raw_own,
             dst_ref=raw_in.at[slot],
             send_sem=raw_send.at[slot],
             recv_sem=raw_recv.at[slot],
             device_id={"col": peer},
         )
+
+    raw_sends = [raw_copy(partner, 0)]
+    raw_sends += [raw_copy(y_at(zh, d), 1 + raw_reach.index(-d)) for d in raw_reach]
+
+    @pl.when(zh == 1)
+    def _():
+        exchange(other_half, in_own, cross_parts, cross_send, cross_recv)
+        raw_sends[0].start()
+
+    await_some(half_here, cols // Z_HI - 1 - rank)
+    exchange(half_peers, in_own, in_parts, in_send, in_recv)
+    for copy in raw_sends[1:]:
         copy.start()
-        raw_sends.append(copy)
-
-    send_raw(partner, 0)
-    in_pair[...] = collect(in_own, pair_part, pair_sem.at[1])
-    exchange(half_peers, in_pair, in_parts, in_send, in_recv)
-    for d in raw_reach:
-        send_raw(y_at(zh, d), 1 + reach.index(-d))
 
     def locate_b(block, carry):
         count = jnp.int32(0)
@@ -192,8 +234,6 @@
             b_slot[block * tr * tc + t] = jnp.where(here > 0, SLOTS * block + count, SLOTS * cols)
             count = count + here
         return carry
-
-    lax.fori_loop(0, cols, locate_b, 0)
 
     def locate_a(block, carry):
         count = jnp.int32(0)
@@ -211,13 +251,33 @@
             a_col[block * SLOTS + s] = tc * (tc * block + col_[s])
         return carry
 
-    lax.fori_loop(0, rows, locate_a, 0)
-
-    raw_origins = [partner, *(y_at(zh, d) for d in reach)]
+    def locate_all():
+        lax.fori_loop(0, cols, locate_b, 0)
+        lax.fori_loop(0, rows, locate_a, 0)
+
     raw_cols = [locate(origin, r)[2] for origin in raw_origins]
-    in_sum = collect(in_pair, in_parts, in_recv)
-    for j in range(tc):
-        in_total[j] = in_sum[:, j * TILE : (j + 1) * TILE]
+    pl.when(zh == 1)(locate_all)
+    in_pair[...] = collect(in_own, in_parts, in_recv)
+
+    @pl.when(zh == 0)
+    def _():
+        pl.semaphore_wait(partner_here, 1)
+        exchange([partner], in_pair, pair_part, pair_sem.at[0], pair_sem.at[1])
+        raw_sends[0].start()
+
+    def set_total(total):
+        for j in range(tc):
+            in_total[j] = total[:, j * TILE : (j + 1) * TILE]
+
+    @pl.when(zh == 0)
+    def _():
+        locate_all()
+        set_total(collect(in_pair, cross_parts, cross_recv))
+
+    @pl.when(zh == 1)
+    def _():
+        set_total(collect(in_pair, pair_part, pair_sem.at[1]))
+
     for s in range(SLOTS):
         stoch = (tiles[s] / in_total[place_col[s]]).astype(jnp.bfloat16)
         a_pack[SLOTS * r + s] = stoch
@@ -264,9 +324,12 @@
     sibling = col_of(zh, y, 1 - core)
     half = y_size // 2
 
+    def others(at, size):
+        return [k + 1 - (at - k + size - 1) // size for k in range(size - 1)]
+
     def around_x(origin, s):
-        for d in (*range(2, x_size - 1), 1, x_size - 1):
-            send_a(origin, s, row_of(zl, (x + d) % x_size))
+        for to in others(x, x_size):
+            send_a(origin, s, row_of(zl, to))
 
     far_count = 0
 
@@ -299,17 +362,18 @@
         wait_b(y_at(zh_, d))
         send_b(y_at(zh_, d), sibling)
 
-    def z_arrival(d, s):
-        origin = row_of((zl + d) % Z_LO, x)
+    def z_arrival(zl_, s):
+        origin = row_of(zl_, x)
         wait_a(origin, s)
         around_x(origin, s)
 
     for d in reach:
         if d not in raw_reach:
             send_b(c, y_at(zh, d))
+    await_some(row_here, Z_LO - 1 - zl + x_size - 1 - x)
     for s in range(SLOTS):
-        for d in (2, 1, 3):
-            send_a(r, s, row_of((zl + d) % Z_LO, x))
+        for to in others(zl, Z_LO):
+            send_a(r, s, row_of(to, x))
     for s in range(SLOTS):
         around_x(r, s)
     send_b(c, sibling)
@@ -317,16 +381,12 @@
     for d in reach:
         send_b(partner, y_at(zh, d))
     send_b(partner, sibling)
-    for n, d in enumerate(reach, 1):
-        if d in raw_reach:
-            raw_arrival(n)
-            if abs(d) == 2:
-                spread(zh, d)
-            else:
-                send_b(raw_origins[n], sibling)
+    for n, d in enumerate(raw_reach, 1):
+        raw_arrival(n)
+        spread(zh, d)
     for s in range(SLOTS):
-        for d in (1, 3, 2):
-            z_arrival(d, s)
+        for zl_ in others(zl, Z_LO):
+            z_arrival(zl_, s)
     for zh_ in (zh, other):
         for d in reach:
             if zh_ is zh and d in raw_reach:
@@ -377,7 +437,7 @@
         )
         return carry
 
-    lax.fori_loop(0, rows, multiply, 0, unroll=4)
+    lax.fori_loop(0, rows, multiply, 0, unroll=16)
 
     sums = []
     for j in range(tc):
@@ -394,7 +454,15 @@
     exchange(all_peers, out_own, out_parts, out_send, out_recv)
     store = pltpu.make_async_copy(result, result_hbm, store_sem.at[0])
     store.start()
-    drain(pair_part, pair_sem.at[0])
+
+    @pl.when(zh == 0)
+    def _():
+        drain(pair_part, pair_sem.at[0])
+
+    @pl.when(zh == 1)
+    def _():
+        drain(cross_parts, cross_send)
+
     for copy in raw_sends:
         copy.wait_send()
     drain(in_parts, in_send)
@@ -432,8 +500,9 @@
             pltpu.SMEM(pattern.shape, jnp.int32),
             pltpu.SMEM(prune.shape, jnp.int32),
             pltpu.VMEM((SLOTS, TILE, TILE), f32),
-            pltpu.VMEM((5, SLOTS, TILE, TILE), f32),
+            pltpu.VMEM((3, SLOTS, TILE, TILE), f32),
             pltpu.VMEM((1, 1, width), f32),
+            pltpu.VMEM((cols // Z_HI, 1, width), f32),
             pltpu.VMEM((1, width), f32),
             pltpu.VMEM((1, width), f32),
             pltpu.VMEM((rows * SLOTS, TILE, TILE), bf16),
@@ -450,9 +519,14 @@
             dma((tr * tc,)),
             dma((2,)),
             dma((2,)),
-            dma((5,)),
-            dma((5,)),
+            dma((3,)),
+            dma((3,)),
             dma((2,)),
+            dma,
+            dma,
+            pltpu.SemaphoreType.REGULAR,
+            pltpu.SemaphoreType.REGULAR,
+            pltpu.SemaphoreType.REGULAR,
             dma((4,)),
             dma((4,)),
             dma,

time: 51.3 us -> 48.5 us (0.945); the launches traced: 50.4 us -> 48.3 us
  Pallas kernels: 49.5 us -> 47.4 us
    pallas_call x1, Pallas kernels: 49.5 us -> 47.4 us  [on_device(): pl.pallas_call(functools.partial(kernel, rows, cols), out_shape=[jax.Shap...]
where the time goes in v4:
time: 48.5 us; the launch traced here: 48.3 us
  Pallas kernels  47.4 us (98%)
  other arithmetic  0.86 us (2%)
    pallas_call x1, Pallas kernels, on_device(): pl.pallas_call(functools.partial(kernel, rows, cols), out_shape=[jax.Shap...  47.4 us

profile of v4, /device:TPU:1, one launch (start us, length us, event | category | flops | bytes accessed | tf_op | source)
XLA Modules:
  0.0 48.3 jit_solution(3403080336349966369)
XLA Ops:
  0.0 47.4 %shard_map.37 = (f32[256,512]{1,0:T(8,128)S(1)}, f32[1,512]{1,0:T(1,128)S(1)}) custom-call(f32[256,512]{1,0:T(8,128)} %values_hbm.1, s32[64,64]{1,0:T(8,128)} %pattern_hbm.1, s32[2,4]{1,0:T(2,128)} %prune_hbm.1), custom_call_target="tpu_custom_call" | custom-call | flops 1073741824 | bytes 1048576 | tf_op jit(solution)/shard_map/pallas_call | solution.py:490
  47.4 0.9 %broadcast_multiply_fusion = f32[256,512]{1,0:T(8,128)} fusion(f32[256,512]{1,0:T(8,128)S(1)} %get-tuple-element.7, f32[512]{0:T(512)S(1)} %bitcast.1), kind=kLoop, calls=%fused_computation | loop fusion | flops 131072 | bytes 1050624 | tf_op jit(solution)/shard_map/mul | solution.py:552

commit v5 on v4

--- a/solution.py
+++ b/solution.py
@@ -95,7 +95,6 @@
     def at_offset(dz, dy, dc):
         return col_of((zh + dz) % Z_HI, (y + dy) % y_size, (core + dc) % CORES)
 
-    all_peers = [at_offset(*o) for o in offsets]
     half_peers = [at_offset(*o) for o in offsets if o[0] == 0]
     other_half = [at_offset(*o) for o in offsets if o[0] == 1]
 
@@ -156,6 +155,8 @@
 
     for copy in fetches:
         copy.wait()
+
+    result[...] = jnp.zeros_like(result)
 
     def locate(block_row, block_col):
         seen = jnp.int32(0)
@@ -385,8 +386,10 @@
         raw_arrival(n)
         spread(zh, d)
     for s in range(SLOTS):
-        for zl_ in others(zl, Z_LO):
+        for zl_ in others(zl, Z_LO)[:-1]:
             z_arrival(zl_, s)
+    for s in range(SLOTS):
+        z_arrival(others(zl, Z_LO)[-1], s)
     for zh_ in (zh, other):
         for d in reach:
             if zh_ is zh and d in raw_reach:
@@ -405,25 +408,19 @@
             pltpu.make_async_copy(tile, tile, far_recv.at[n + s]).wait()
         send_b(origin, sibling)
 
-    for zl_ in range(Z_LO):
-        for d in range(1, x_size):
-            for s in range(SLOTS):
-                wait_a(row_of((zl + zl_) % Z_LO, (x + d) % x_size), s)
-
     def wait_sibling(block, carry):
         wait_b(block * CORES + 1 - core)
         return carry
 
     lax.fori_loop(0, cols // CORES, wait_sibling, 0)
 
-    result[...] = jnp.zeros_like(result)
-
-    def multiply(block, carry):
+    def multiply(line):
         left, right = [], []
-        for s in range(SLOTS):
-            row_ = a_row[block * SLOTS + s]
-            k = a_col[block * SLOTS + s]
-            tile = a_pack[block * SLOTS + s]
+        for n in range(x_size * SLOTS):
+            slot = line * x_size * SLOTS + n
+            row_ = a_row[slot]
+            k = a_col[slot]
+            tile = a_pack[slot]
             left.append(
                 jnp.concatenate(
                     [jnp.where(row_ == i, tile, jnp.zeros_like(tile)) for i in range(tr)], axis=0
@@ -435,9 +432,12 @@
             jnp.concatenate(right, axis=0),
             preferred_element_type=jnp.float32,
         )
-        return carry
-
-    lax.fori_loop(0, rows, multiply, 0, unroll=16)
+
+    for line in (zl, *others(zl, Z_LO)):
+        for d in range(1, x_size):
+            for s in range(SLOTS):
+                wait_a(row_of(line, (x + d) % x_size), s)
+        multiply(line)
 
     sums = []
     for j in range(tc):
@@ -451,7 +451,15 @@
         sums.append(col_sum)
     out_own[...] = jnp.concatenate(sums, axis=1)
 
-    exchange(all_peers, out_own, out_parts, out_send, out_recv)
+    for k in range(cols - 1):
+        below = (c - k + cols - 1) // cols
+        pltpu.make_async_remote_copy(
+            src_ref=out_own,
+            dst_ref=out_parts.at[c - below],
+            send_sem=out_send,
+            recv_sem=out_recv,
+            device_id={"col": k + 1 - below},
+        ).start()
     store = pltpu.make_async_copy(result, result_hbm, store_sem.at[0])
     store.start()
 

time: 48.5 us -> 47.4 us (0.977)
  Pallas kernels: 47.4 us -> 46.3 us
    pallas_call x1, Pallas kernels: 47.4 us -> 46.3 us  [on_device(): pl.pallas_call(functools.partial(kernel, rows, cols), out_shape=[jax.Shap...]
where the time goes in v5:
time: 47.4 us; the launch traced here: 47.2 us
  Pallas kernels  46.3 us (98%)
  other arithmetic  0.86 us (2%)
    pallas_call x1, Pallas kernels, on_device(): pl.pallas_call(functools.partial(kernel, rows, cols), out_shape=[jax.Shap...  46.3 us

profile of v5, /device:TPU:1, one launch (start us, length us, event | category | flops | bytes accessed | tf_op | source)
XLA Modules:
  0.0 47.2 jit_solution(8322336027518785116)
XLA Ops:
  0.0 46.3 %shard_map.37 = (f32[256,512]{1,0:T(8,128)S(1)}, f32[1,512]{1,0:T(1,128)S(1)}) custom-call(f32[256,512]{1,0:T(8,128)} %values_hbm.1, s32[64,64]{1,0:T(8,128)} %pattern_hbm.1, s32[2,4]{1,0:T(2,128)} %prune_hbm.1), custom_call_target="tpu_custom_call" | custom-call | flops 1073741824 | bytes 1048576 | tf_op jit(solution)/shard_map/pallas_call | solution.py:498
  46.3 0.9 %broadcast_multiply_fusion = f32[256,512]{1,0:T(8,128)} fusion(f32[256,512]{1,0:T(8,128)S(1)} %get-tuple-element.7, f32[512]{0:T(512)S(1)} %bitcast.1), kind=kLoop, calls=%fused_computation | loop fusion | flops 131072 | bytes 1050624 | tf_op jit(solution)/shard_map/mul | solution.py:560

commit v6 on v5

--- a/solution.py
+++ b/solution.py
@@ -414,10 +414,10 @@
 
     lax.fori_loop(0, cols // CORES, wait_sibling, 0)
 
-    def multiply(line):
+    def multiply(block):
         left, right = [], []
-        for n in range(x_size * SLOTS):
-            slot = line * x_size * SLOTS + n
+        for n in range(SLOTS):
+            slot = block * SLOTS + n
             row_ = a_row[slot]
             k = a_col[slot]
             tile = a_pack[slot]
@@ -434,10 +434,12 @@
         )
 
     for line in (zl, *others(zl, Z_LO)):
-        for d in range(1, x_size):
-            for s in range(SLOTS):
-                wait_a(row_of(line, (x + d) % x_size), s)
-        multiply(line)
+        for d in (0, 1, x_size - 1, *range(2, x_size - 1)):
+            block = row_of(line, (x + d) % x_size)
+            if d:
+                for s in range(SLOTS):
+                    wait_a(block, s)
+            multiply(block)
 
     sums = []
     for j in range(tc):

time: 47.4 us -> 47.7 us (level)
  no operation moved by 1% of the time
where the time goes in v6:
time: 47.7 us; the launch traced here: 47.5 us
  Pallas kernels  46.6 us (98%)
  other arithmetic  0.86 us (2%)
    pallas_call x1, Pallas kernels, on_device(): pl.pallas_call(functools.partial(kernel, rows, cols), out_shape=[jax.Shap...  46.6 us

profile of v6, /device:TPU:1, one launch (start us, length us, event | category | flops | bytes accessed | tf_op | source)
XLA Modules:
  0.0 47.5 jit_solution(3637412064906041051)
XLA Ops:
  0.0 46.6 %shard_map.37 = (f32[256,512]{1,0:T(8,128)S(1)}, f32[1,512]{1,0:T(1,128)S(1)}) custom-call(f32[256,512]{1,0:T(8,128)} %values_hbm.1, s32[64,64]{1,0:T(8,128)} %pattern_hbm.1, s32[2,4]{1,0:T(2,128)} %prune_hbm.1), custom_call_target="tpu_custom_call" | custom-call | flops 1073741824 | bytes 1048576 | tf_op jit(solution)/shard_map/pallas_call | solution.py:500
  46.6 0.9 %broadcast_multiply_fusion = f32[256,512]{1,0:T(8,128)} fusion(f32[256,512]{1,0:T(8,128)S(1)} %get-tuple-element.7, f32[512]{0:T(512)S(1)} %bitcast.1), kind=kLoop, calls=%fused_computation | loop fusion | flops 131072 | bytes 1050624 | tf_op jit(solution)/shard_map/mul | solution.py:562
